TPU v7x, 32 devices: a whole 2x2x4 slice. The times are simulated.
32 devices in a mesh: az: 8 (over y, x, core), rad: 4 (over z).
Axes of the slice: x: 2, y: 2, z: 4, core: 2. Of those that a mesh axis runs over, the one named last changes fastest.
Arguments:
- block_mass: float32 [8, 4, 512, 128], P('az', 'rad'), may hold values from 0.5 to 4
- block_flux: float32 [8, 4, 512, 9, 128], P('az', 'rad'), may hold values from -6 to 6
- block_dest: int32 [8, 4, 512], P('az', 'rad'), may hold values from 0 to 2047, as said below
- block_count: int32 [8, 4], P('az', 'rad'), may hold values from 128 to 512, as said below
Outputs:
- smoothed: float32 [10, 64, 32, 512], P(None, 'az', None, 'rad')
- force: float32 [3, 64, 32, 512], P(None, 'az', None, 'rad')
- strain: float32 [6, 64, 32, 512], P(None, 'az', None, 'rad')
Inputs may be any that keep to these rules, and one draw needn't show every extreme that they name: `block_dest`: the azimuthal row of a block of device (a, b) lies from 2 rows before to 2 rows after the rows a * 8 to a * 8 + 7, cyclically over 64 rows. `block_count`: some device is full in every draw.
All inputs are finite; a program needn't handle non-finite values.
Results may differ from a plain program's by a relative error of at most 0.000076.
Values sent between devices are 32-bit elements; how exact they have to be, the bound alone decides.
A program may use at most 64 MiB of HBM per device.

v0:
```python
import math

import jax
import jax.numpy as jnp
from jax import lax
from jax.sharding import PartitionSpec as P

CA = 8
H = 32


density_base = 0.5


def passed_along(value, axis, steps):
    count = lax.axis_size(axis)
    pairs = [(source, (source + steps) % count) for source in range(count)]
    return lax.ppermute(value, axis, pairs)


def padded_2(cells, sides, width):
    for axis, dim in sides:
        count = lax.axis_size(axis)
        head = lax.slice_in_dim(cells, 0, width, axis=dim)
        tail = lax.slice_in_dim(cells, cells.shape[dim] - width, cells.shape[dim], axis=dim)
        cells = jnp.concatenate(
            [
                lax.ppermute(tail, axis, [(i, (i + 1) % count) for i in range(count)]),
                cells,
                lax.ppermute(head, axis, [((i + 1) % count, i) for i in range(count)]),
            ],
            axis=dim,
        )
    return cells


def smooth_block(extended):
    fields = 0.25 * extended[:, :-2] + 0.5 * extended[:, 1:-1] + 0.25 * extended[:, 2:]
    fields = 0.25 * fields[..., :-2] + 0.5 * fields[..., 1:-1] + 0.25 * fields[..., 2:]
    padded = jnp.pad(fields, ((0, 0), (0, 0), (1, 1), (0, 0)))
    return 0.25 * padded[:, :, :-2] + 0.5 * padded[:, :, 1:-1] + 0.25 * padded[:, :, 2:]


def radial_mask(extended, depth, band_index, width, n_rad):
    columns = band_index * width - depth + jnp.arange(width + 2 * depth, dtype=jnp.int32)
    inside = (columns >= 0) & (columns < width * n_rad)
    return extended * inside.astype(jnp.float32)


def gradients(extended, scale_az):
    center = extended[:, 1:-1, :, 1:-1]
    grad_az = (extended[:, 2:, :, 1:-1] - extended[:, :-2, :, 1:-1]) * scale_az
    grad_rad = (extended[:, 1:-1, :, 2:] - extended[:, 1:-1, :, :-2]) * 0.5
    padded = jnp.pad(center, ((0, 0), (0, 0), (1, 1), (0, 0)))
    grad_height = (padded[:, :, 2:] - padded[:, :, :-2]) * 0.5
    return (grad_az, grad_height, grad_rad, center)


def assemble(grad_az, grad_height, grad_rad, center, recip):
    force = jnp.stack(
        [
            grad_az[3] + grad_height[6] + grad_rad[7] + 2.0 * center[7] * recip,
            grad_az[6] + grad_height[4] + grad_rad[8],
            grad_az[7] + grad_height[8] + grad_rad[5] + (center[5] - center[3]) * recip,
        ]
    )
    strain = jnp.stack(
        [
            grad_az[0] + center[2] * recip,
            grad_height[1],
            grad_rad[2],
            0.5 * (grad_height[0] + grad_az[1]),
            0.5 * (grad_rad[0] + grad_az[2] - center[0] * recip),
            0.5 * (grad_rad[1] + grad_height[2]),
        ]
    )
    return (force, strain)


def deposit(onehot, values):
    return jnp.einsum("ls,scn->cln", onehot, values, precision=lax.Precision.HIGHEST)


def local_rows(values, dest, live, start, total_rows, width):
    local_row = jnp.mod(dest // H - start + 2, total_rows)
    line = local_row * H + dest % H
    onehot = (
        (jnp.arange((CA + 4) * H, dtype=jnp.int32)[:, None] == line[None, :]) & live[None, :]
    ).astype(jnp.float32)
    return deposit(onehot, values).reshape(10, CA + 4, H, width)


def local(block_mass, block_flux, block_dest, block_count):
    sector = lax.axis_index("az")
    band_index = lax.axis_index("rad")
    n_az = lax.axis_size("az")
    n_rad = lax.axis_size("rad")
    slots = block_mass.shape[2]
    width = block_mass.shape[3]
    total_rows = CA * n_az
    start = sector * CA
    values = jnp.concatenate([block_mass[0, 0][:, None, :], block_flux[0, 0]], axis=1)
    dest = block_dest[0, 0]
    slot_index = jnp.arange(slots, dtype=jnp.int32)
    live = slot_index < block_count[0, 0]
    extended = local_rows(values, dest, live, start, total_rows, width)
    from_left = passed_along(extended[:, CA + 2 :], "az", 1)
    from_right = passed_along(extended[:, :2], "az", -1)
    fields = extended[:, 2 : CA + 2]
    fields = fields.at[:, :2].add(from_left)
    fields = fields.at[:, CA - 2 :].add(from_right)
    glob_cells = (band_index * width + jnp.arange(width, dtype=jnp.int32)).astype(jnp.float32)
    radius = width * n_rad + glob_cells + 0.5
    dtheta = 2.0 * math.pi / total_rows
    scale_az = 0.5 / (radius * dtheta)
    recip = 1.0 / radius
    extended = padded_2(fields, (("az", 1), ("rad", 3)), 1)
    extended = radial_mask(extended, 1, band_index, width, n_rad)
    smoothed = smooth_block(extended)
    velocity = smoothed[1:4] / (smoothed[0:1] + density_base)
    combined = jnp.concatenate([velocity, smoothed[4:]], axis=0)
    outer = padded_2(combined, (("az", 1), ("rad", 3)), 1)
    outer = radial_mask(outer, 1, band_index, width, n_rad)
    grad_az, grad_height, grad_rad, center = gradients(outer, scale_az)
    force, strain = assemble(grad_az, grad_height, grad_rad, center, recip)
    return (smoothed, force, strain)


def solution(mesh):
    return jax.shard_map(
        local,
        mesh=mesh,
        in_specs=(
            P("az", "rad", None, None),
            P("az", "rad", None, None, None),
            P("az", "rad", None),
            P("az", "rad"),
        ),
        out_specs=(
            P(None, "az", None, "rad"),
            P(None, "az", None, "rad"),
            P(None, "az", None, "rad"),
        ),
        check_vma=False,
    )
```

profile of v0, /device:TPU:0, one launch (start us, length us, event | category | flops | bytes accessed | tf_op | source)
XLA Modules:
  0.0 76.7 jit_solution(3959268076982083987)
XLA Ops:
  1.3 1.1 %copy.16 = f32[1,1,512,128]{2,3,1,0:T(8,128)S(1)} copy(f32[1,1,512,128]{3,2,1,0:T(8,128)} %param.8) | data formatting | bytes 524288 | tf_op args[0]
  2.4 2.1 %copy.17 = f32[1,1,512,9,128]{2,4,3,1,0:T(8,128)S(1)} copy(f32[1,1,512,9,128]{4,2,3,1,0:T(8,128)} %param.9) | data formatting | bytes 4718592 | tf_op args[1]
  4.5 3.5 %fusion.6 = f32[10,384,128]{1,2,0:T(8,128)} fusion(f32[512,9,128]{0,2,1:T(8,128)S(1)} %bitcast.13, f32[512,1,128]{0,2,1:T(8,128)S(1)} %bitcast.17, s32[512]{0:T(512)S(1)} %fusion.42, pred[512]{0:T(512)(128)(4,1)S(1)} %iota_compare_fusion.1), kind=kOutput, calls=%fused_computation.14 | convolution fusion | flops 3020947456 | bytes 4590080 | tf_op jit(solution)/shard_map/ls,scn->cln/dot_general | solution.py:81
  8.0 1.9 %copy.18 = f32[10,384,128]{2,1,0:T(8,128)S(1)} copy(f32[10,384,128]{1,2,0:T(8,128)} %fusion.6) | data formatting | bytes 3932160 | tf_op jit(solution)/shard_map/ls,scn->cln/transpose | solution.py:81
  10.5 2.9 %collective-permute-start.1 = (f32[10,2,32,128]{3,2,1,0:T(8,128)S(1)}, f32[10,2,32,128]{3,2,1,0:T(8,128)S(1)}, u32[]{:S(2)}, u32[]{:S(2)}) collective-permute-start(f32[10,2,32,128]{3,2,1,0:T(8,128)S(1)} %get-tuple-element.36), channel_id=1, source_target_pairs={{0,28},{4,0},{8,4},{12,8},{16,12},{20,16},{24,20},{28,24},{1,29},{... | collective-permute-start | bytes 983048 | tf_op jit(solution)/shard_map/ppermute | solution.py:18
  13.5 5.4 %collective-permute-done = f32[10,2,32,128]{3,2,1,0:T(8,128)S(1)} collective-permute-done((f32[10,2,32,128]{3,2,1,0:T(8,128)S(1)}, f32[10,2,32,128]{3,2,1,0:T(8,128)S(1)}, u32[]{:S(2)}, u32[]{:S(2)}) %collective-permute-start) | collective-permute-done | bytes 327712 | tf_op jit(solution)/shard_map/ppermute | solution.py:18
  19.0 1.5 %collective-permute-done.1 = f32[10,2,32,128]{3,2,1,0:T(8,128)S(1)} collective-permute-done((f32[10,2,32,128]{3,2,1,0:T(8,128)S(1)}, f32[10,2,32,128]{3,2,1,0:T(8,128)S(1)}, u32[]{:S(2)}, u32[]{:S(2)}) %collective-permute-start.1) | collective-permute-done | bytes 327712 | tf_op jit(solution)/shard_map/ppermute | solution.py:18
  20.7 2.9 %collective-permute-start.3 = (f32[10,1,32,128]{3,2,1,0:T(8,128)S(1)}, f32[10,1,32,128]{3,2,1,0:T(8,128)S(1)}, u32[]{:S(2)}, u32[]{:S(2)}) collective-permute-start(f32[10,1,32,128]{3,2,1,0:T(8,128)S(1)} %slice.282), channel_id=1, source_target_pairs={{4,0},{8,4},{12,8},{16,12},{20,16},{24,20},{28,24},{0,28},{5,1},{9... | collective-permute-start | bytes 491528 | tf_op jit(solution)/shard_map/ppermute | solution.py:30
  23.5 4.6 %collective-permute-done.3 = f32[10,1,32,128]{3,2,1,0:T(8,128)S(1)} collective-permute-done((f32[10,1,32,128]{3,2,1,0:T(8,128)S(1)}, f32[10,1,32,128]{3,2,1,0:T(8,128)S(1)}, u32[]{:S(2)}, u32[]{:S(2)}) %collective-permute-start.3) | collective-permute-done | bytes 163872 | tf_op jit(solution)/shard_map/ppermute | solution.py:30
  29.3 1.8 %fusion.47 = (f32[10,10,32,1]{3,2,1,0:T(8,128)}, f32[10,10,32,1]{3,2,1,0:T(8,128)S(1)}) fusion(f32[10,10,32,128]{3,2,1,0:T(8,128)S(1)} %pad_maximum_fusion), kind=kLoop, calls=%fused_computation.98 | loop fusion | bytes 51200 | tf_op jit(solution)/shard_map/slice | solution.py:25
  31.1 2.1 %copy.19 = f32[10,10,32,1]{2,3,1,0:T(1,128)S(1)} copy(f32[10,10,32,1]{3,2,1,0:T(8,128)} %get-tuple-element.38) | data formatting | bytes 25600 | tf_op jit(solution)/shard_map/slice | solution.py:25
  33.8 3.9 %collective-permute-start.5 = (f32[10,10,32,1]{2,3,1,0:T(1,128)S(1)}, f32[10,10,32,1]{2,3,1,0:T(1,128)S(1)}, u32[]{:S(2)}, u32[]{:S(2)}) collective-permute-start(f32[10,10,32,1]{2,3,1,0:T(1,128)S(1)} %copy.20), channel_id=1, source_target_pairs={{1,0},{2,1},{3,2},{0,3},{5,4},{6,5},{7,6},{4,7},{9,8},{10,9},{11,1... | collective-permute-start | bytes 38408 | tf_op jit(solution)/shard_map/ppermute | solution.py:30
  37.7 5.9 %collective-permute-done.4 = f32[10,10,32,1]{2,3,1,0:T(1,128)S(1)} collective-permute-done((f32[10,10,32,1]{2,3,1,0:T(1,128)S(1)}, f32[10,10,32,1]{2,3,1,0:T(1,128)S(1)}, u32[]{:S(2)}, u32[]{:S(2)}) %collective-permute-start.4) | collective-permute-done | bytes 12832 | tf_op jit(solution)/shard_map/ppermute | solution.py:28
  44.3 1.8 %copy.22 = f32[10,10,32,1]{3,2,1,0:T(8,128)} copy(f32[10,10,32,1]{2,3,1,0:T(1,128)S(1)} %collective-permute-done.5) | data formatting | bytes 25600 | tf_op jit(solution)/shard_map/ppermute | solution.py:30
  46.1 2.8 %maximum_multiply_fusion = f32[10,10,32,130]{3,2,1,0:T(8,128)S(1)} fusion(f32[10,10,32,1]{3,2,1,0:T(8,128)} %copy.22, f32[10,1,32,128]{3,2,1,0:T(8,128)S(1)} %collective-permute-done.3, f32[10,8,32,128]{3,2,1,0:T(8,128)S(1)} %get-tuple-element.27, f32[10,1,32,128]{3,2,1,0:T(8,128)S(1)} %collective-permute-done.2, f32[10,10,32,1]{3,2,1,0:T(8,128)S(1)} %copy.21, ...), kind=kLoop, calls=%fused_computation | loop fusion | flops 2080000 | bytes 3328520 | tf_op jit(solution)/shard_map/mul | solution.py:47
  51.7 2.6 %collective-permute-start.7 = (f32[9,1,32,128]{3,2,1,0:T(8,128)S(1)}, f32[9,1,32,128]{3,2,1,0:T(8,128)S(1)}, u32[]{:S(2)}, u32[]{:S(2)}) collective-permute-start(f32[9,1,32,128]{3,2,1,0:T(8,128)S(1)} %get-tuple-element.43), channel_id=1, source_target_pairs={{4,0},{8,4},{12,8},{16,12},{20,16},{24,20},{28,24},{0,28},{5,1},{9... | collective-permute-start | bytes 442376 | tf_op jit(solution)/shard_map/ppermute | solution.py:30
  54.4 3.9 %collective-permute-done.6 = f32[9,1,32,128]{3,2,1,0:T(8,128)S(1)} collective-permute-done((f32[9,1,32,128]{3,2,1,0:T(8,128)S(1)}, f32[9,1,32,128]{3,2,1,0:T(8,128)S(1)}, u32[]{:S(2)}, u32[]{:S(2)}) %collective-permute-start.6) | collective-permute-done | bytes 147488 | tf_op jit(solution)/shard_map/ppermute | solution.py:28
  58.4 1.7 %fusion.48 = (f32[9,10,32,1]{3,2,1,0:T(8,128)}, f32[9,10,32,1]{3,2,1,0:T(8,128)S(1)}) fusion(f32[9,10,32,128]{3,2,1,0:T(8,128)S(1)} %pad_maximum_fusion.1), kind=kLoop, calls=%fused_computation.99 | loop fusion | bytes 46080 | tf_op jit(solution)/shard_map/slice | solution.py:25
  60.0 2.0 %copy.23 = f32[9,10,32,1]{2,3,1,0:T(1,128)S(1)} copy(f32[9,10,32,1]{3,2,1,0:T(8,128)} %get-tuple-element.40) | data formatting | bytes 23040 | tf_op jit(solution)/shard_map/slice | solution.py:25
  62.6 2.0 %collective-permute-start.8 = (f32[9,10,32,1]{2,3,1,0:T(1,128)S(1)}, f32[9,10,32,1]{2,3,1,0:T(1,128)S(1)}, u32[]{:S(2)}, u32[]{:S(2)}) collective-permute-start(f32[9,10,32,1]{2,3,1,0:T(1,128)S(1)} %copy.23), channel_id=1, source_target_pairs={{0,1},{1,2},{2,3},{3,0},{4,5},{5,6},{6,7},{7,4},{8,9},{9,10},{10,1... | collective-permute-start | bytes 34568 | tf_op jit(solution)/shard_map/ppermute | solution.py:28
  64.7 4.1 %collective-permute-done.8 = f32[9,10,32,1]{2,3,1,0:T(1,128)S(1)} collective-permute-done((f32[9,10,32,1]{2,3,1,0:T(1,128)S(1)}, f32[9,10,32,1]{2,3,1,0:T(1,128)S(1)}, u32[]{:S(2)}, u32[]{:S(2)}) %collective-permute-start.8) | collective-permute-done | bytes 11552 | tf_op jit(solution)/shard_map/ppermute | solution.py:28
  69.3 1.7 %copy.26 = f32[9,10,32,1]{3,2,1,0:T(8,128)} copy(f32[9,10,32,1]{2,3,1,0:T(1,128)S(1)} %collective-permute-done.9) | data formatting | bytes 23040 | tf_op jit(solution)/shard_map/ppermute | solution.py:30
  71.1 2.6 %maximum_multiply_fusion.1 = f32[9,10,32,130]{3,2,1,0:T(8,128)S(1)} fusion(f32[9,10,32,1]{3,2,1,0:T(8,128)} %copy.26, f32[9,1,32,128]{3,2,1,0:T(8,128)S(1)} %collective-permute-done.7, f32[6,8,32,128]{3,2,1,0:T(8,128)S(1)} %slice.293, f32[3,8,32,128]{3,2,1,0:T(8,128)S(1)} %slice_divide_fusion, f32[9,1,32,128]{3,2,1,0:T(8,128)S(1)} %collective-permute-done.6, ...), kind=kLoop, calls=%fused_computation.1 | loop fusion | flops 2246400 | bytes 2995720 | tf_op jit(solution)/shard_map/mul | solution.py:47
  73.7 1.3 %fusion.18 = (f32[9,8,32,128]{3,2,1,0:T(8,128)S(1)}, f32[9,8,32,128]{3,2,1,0:T(8,128)S(1)}, f32[9,8,32,128]{3,2,1,0:T(8,128)S(1)}) fusion(f32[9,10,32,130]{3,2,1,0:T(8,128)S(1)} %maximum_multiply_fusion.1, f32[128]{0:T(128)S(1)} %get-tuple-element.44), kind=kLoop, calls=%fused_computation.32 | loop fusion | flops 1179648 | bytes 9437696 | tf_op jit(solution)/shard_map/mul | solution.py:52
  (47 shorter events, 9.3 us)
Async XLA Ops:
  2.4 2.1 %copy-start.2 = (s32[1,1,512]{2,1,0:T(1,128)S(1)}, s32[1,1,512]{2,1,0:T(1,128)}, u32[]{:S(2)}) copy-start(s32[1,1,512]{2,1,0:T(1,128)} %param.10) | copy-start | bytes 6148
  10.0 9.0 %collective-permute-start = (f32[10,2,32,128]{3,2,1,0:T(8,128)S(1)}, f32[10,2,32,128]{3,2,1,0:T(8,128)S(1)}, u32[]{:S(2)}, u32[]{:S(2)}) collective-permute-start(f32[10,2,32,128]{3,2,1,0:T(8,128)S(1)} %get-tuple-element.37), channel_id=1, source_target_pairs={{0,4},{4,8},{8,12},{12,16},{16,20},{20,24},{24,28},{28,0},{1,5},{5... | collective-permute-start | bytes 983048 | tf_op jit(solution)/shard_map/ppermute | solution.py:18
  10.5 10.0 %collective-permute-start.1 = (f32[10,2,32,128]{3,2,1,0:T(8,128)S(1)}, f32[10,2,32,128]{3,2,1,0:T(8,128)S(1)}, u32[]{:S(2)}, u32[]{:S(2)}) collective-permute-start(f32[10,2,32,128]{3,2,1,0:T(8,128)S(1)} %get-tuple-element.36), channel_id=1, source_target_pairs={{0,28},{4,0},{8,4},{12,8},{16,12},{20,16},{24,20},{28,24},{1,29},{... | collective-permute-start | bytes 983048 | tf_op jit(solution)/shard_map/ppermute | solution.py:18
  20.7 7.4 %collective-permute-start.3 = (f32[10,1,32,128]{3,2,1,0:T(8,128)S(1)}, f32[10,1,32,128]{3,2,1,0:T(8,128)S(1)}, u32[]{:S(2)}, u32[]{:S(2)}) collective-permute-start(f32[10,1,32,128]{3,2,1,0:T(8,128)S(1)} %slice.282), channel_id=1, source_target_pairs={{4,0},{8,4},{12,8},{16,12},{20,16},{24,20},{28,24},{0,28},{5,1},{9... | collective-permute-start | bytes 491528 | tf_op jit(solution)/shard_map/ppermute | solution.py:30
  23.5 5.6 %collective-permute-start.2 = (f32[10,1,32,128]{3,2,1,0:T(8,128)S(1)}, f32[10,1,32,128]{3,2,1,0:T(8,128)S(1)}, u32[]{:S(2)}, u32[]{:S(2)}) collective-permute-start(f32[10,1,32,128]{3,2,1,0:T(8,128)S(1)} %slice.281), channel_id=1, source_target_pairs={{0,4},{4,8},{8,12},{12,16},{16,20},{20,24},{24,28},{28,0},{1,5},{5... | collective-permute-start | bytes 491528 | tf_op jit(solution)/shard_map/ppermute | solution.py:28
  33.8 10.5 %collective-permute-start.5 = (f32[10,10,32,1]{2,3,1,0:T(1,128)S(1)}, f32[10,10,32,1]{2,3,1,0:T(1,128)S(1)}, u32[]{:S(2)}, u32[]{:S(2)}) collective-permute-start(f32[10,10,32,1]{2,3,1,0:T(1,128)S(1)} %copy.20), channel_id=1, source_target_pairs={{1,0},{2,1},{3,2},{0,3},{5,4},{6,5},{7,6},{4,7},{9,8},{10,9},{11,1... | collective-permute-start | bytes 38408 | tf_op jit(solution)/shard_map/ppermute | solution.py:30
  37.7 5.9 %collective-permute-start.4 = (f32[10,10,32,1]{2,3,1,0:T(1,128)S(1)}, f32[10,10,32,1]{2,3,1,0:T(1,128)S(1)}, u32[]{:S(2)}, u32[]{:S(2)}) collective-permute-start(f32[10,10,32,1]{2,3,1,0:T(1,128)S(1)} %copy.19), channel_id=1, source_target_pairs={{0,1},{1,2},{2,3},{3,0},{4,5},{5,6},{6,7},{7,4},{8,9},{9,10},{10,1... | collective-permute-start | bytes 38408 | tf_op jit(solution)/shard_map/ppermute | solution.py:28
  50.7 1.1 %copy-start = (f32[10,8,32,128]{3,2,1,0:T(8,128)}, f32[10,8,32,128]{3,2,1,0:T(8,128)S(1)}, u32[]{:S(2)}) copy-start(f32[10,8,32,128]{3,2,1,0:T(8,128)S(1)} %fusion.11) | copy-start | bytes 3932164
  51.7 6.5 %collective-permute-start.6 = (f32[9,1,32,128]{3,2,1,0:T(8,128)S(1)}, f32[9,1,32,128]{3,2,1,0:T(8,128)S(1)}, u32[]{:S(2)}, u32[]{:S(2)}) collective-permute-start(f32[9,1,32,128]{3,2,1,0:T(8,128)S(1)} %get-tuple-element.42), channel_id=1, source_target_pairs={{0,4},{4,8},{8,12},{12,16},{16,20},{20,24},{24,28},{28,0},{1,5},{5... | collective-permute-start | bytes 442376 | tf_op jit(solution)/shard_map/ppermute | solution.py:28
  51.7 6.5 %collective-permute-start.7 = (f32[9,1,32,128]{3,2,1,0:T(8,128)S(1)}, f32[9,1,32,128]{3,2,1,0:T(8,128)S(1)}, u32[]{:S(2)}, u32[]{:S(2)}) collective-permute-start(f32[9,1,32,128]{3,2,1,0:T(8,128)S(1)} %get-tuple-element.43), channel_id=1, source_target_pairs={{4,0},{8,4},{12,8},{16,12},{20,16},{24,20},{28,24},{0,28},{5,1},{9... | collective-permute-start | bytes 442376 | tf_op jit(solution)/shard_map/ppermute | solution.py:30
  62.6 6.7 %collective-permute-start.9 = (f32[9,10,32,1]{2,3,1,0:T(1,128)S(1)}, f32[9,10,32,1]{2,3,1,0:T(1,128)S(1)}, u32[]{:S(2)}, u32[]{:S(2)}) collective-permute-start(f32[9,10,32,1]{2,3,1,0:T(1,128)S(1)} %copy.24), channel_id=1, source_target_pairs={{1,0},{2,1},{3,2},{0,3},{5,4},{6,5},{7,6},{4,7},{9,8},{10,9},{11,1... | collective-permute-start | bytes 34568 | tf_op jit(solution)/shard_map/ppermute | solution.py:30
  62.6 6.1 %collective-permute-start.8 = (f32[9,10,32,1]{2,3,1,0:T(1,128)S(1)}, f32[9,10,32,1]{2,3,1,0:T(1,128)S(1)}, u32[]{:S(2)}, u32[]{:S(2)}) collective-permute-start(f32[9,10,32,1]{2,3,1,0:T(1,128)S(1)} %copy.23), channel_id=1, source_target_pairs={{0,1},{1,2},{2,3},{3,0},{4,5},{5,6},{6,7},{7,4},{8,9},{9,10},{10,1... | collective-permute-start | bytes 34568 | tf_op jit(solution)/shard_map/ppermute | solution.py:28
  75.7 1.0 %copy-start.1 = (f32[6,8,32,128]{3,2,1,0:T(8,128)}, f32[6,8,32,128]{3,2,1,0:T(8,128)S(1)}, u32[]{:S(2)}) copy-start(f32[6,8,32,128]{3,2,1,0:T(8,128)S(1)} %fusion.26) | copy-start | bytes 2359300
where the time goes:
time: 77 us; the launch traced here: 76.7 us
  waiting for transfers between devices  26.4 us (34%)
  local copies, waits for them, and re-layouts  19.9 us (26%)
  starting transfers between devices  14.9 us (19%)
  other arithmetic  10.4 us (14%)
  matrix products  3.53 us (5%)
  between operations  1.53 us (2%)
    ppermute x4, waiting for transfers between devices, padded_2(): lax.ppermute(tail, axis, [(i, (i + 1) % count) for i in range(count)])  14.9 us
    ppermute x4, starting transfers between devices, padded_2(): lax.ppermute(head, axis, [((i + 1) % count, i) for i in range(count)])  9.42 us
    slice x5, local copies, waits for them, and re-layouts, padded_2(): lax.slice_in_dim(cells, cells.shape[dim] - width, cells.shape[dim], axis=...  7.45 us
    ppermute x2, waiting for transfers between devices, passed_along(): return lax.ppermute(value, axis, pairs)  6.92 us
    mul x2, other arithmetic, radial_mask(): return extended * inside.astype(jnp.float32)  5.34 us
    ppermute x4, waiting for transfers between devices, padded_2(): lax.ppermute(head, axis, [((i + 1) % count, i) for i in range(count)])  4.58 us
    unnamed x10, local copies, waits for them, and re-layouts  4.23 us
    ppermute x2, local copies, waits for them, and re-layouts, padded_2(): lax.ppermute(head, axis, [((i + 1) % count, i) for i in range(count)])  3.59 us
  transfers between devices with their start and end apart: 10, of which 7 were waited for; matrix products, arithmetic and copies ran while one was open for 2% of the time, Pallas kernels for 0%

commit v1 on v0

v1 whole, which is shorter than its diff:
```python
import functools
import math

import jax
import jax.numpy as jnp
from jax import lax
from jax.experimental import pallas as pl
from jax.experimental.pallas import tpu as pltpu
from jax.sharding import PartitionSpec as P

CA = 8
H = 32
CHANNELS = 10
ROWS = CA + 6
LINES = ROWS * H
SEND = 4 * H

density_base = 0.5

WIDE = (0, 1, 2, 3, 4, 7, 8)
ORDER = (0, 1, 2, 3, 4, 7, 8, 5, 6, 9)
FIRST = 4

MESH = pl.DeviceIdType.MESH


def split(value):
    high = value.astype(jnp.bfloat16)
    low = (value - high.astype(jnp.float32)).astype(jnp.bfloat16)
    return high, low


def kernel(
    n_az, n_rad, count_ref, dest_ref, mass_ref, flux_ref,
    smoothed_ref, force_ref, strain_ref,
    vin, high, low, weights, part, from_left, from_right,
    strip, strip_left, strip_right, edge_out, edge_left, edge_right,
    load_sem, send_sem, recv_sem, band_send, band_recv,
):
    sector = lax.axis_index("az")
    band = lax.axis_index("rad")
    slots = vin.shape[1]
    width = vin.shape[2]
    total_rows = CA * n_az
    right, left = lax.rem(sector + 1, n_az), lax.rem(sector + n_az - 1, n_az)
    outer, inner = band + 1, band - 1
    has_outer, has_inner = band < n_rad - 1, band > 0

    loads = []
    for c in range(CHANNELS):
        source = mass_ref if c == 0 else flux_ref.at[c - 1]
        copy = pltpu.make_async_copy(source, vin.at[c], load_sem.at[c])
        copy.start()
        loads.append(copy)

    barrier = pltpu.get_barrier_semaphore()
    for neighbour in (left, right):
        pl.semaphore_signal(barrier, inc=1, device_id={"az": neighbour}, device_id_type=MESH)

    @pl.when(has_outer)
    def _():
        pl.semaphore_signal(barrier, inc=1, device_id={"rad": outer}, device_id_type=MESH)

    @pl.when(has_inner)
    def _():
        pl.semaphore_signal(barrier, inc=1, device_id={"rad": inner}, device_id_type=MESH)

    dest = dest_ref[...]
    live = lax.broadcasted_iota(jnp.int32, (1, slots), 1) < count_ref[0, 0]
    height = dest & (H - 1)
    offset = (dest >> 5) - sector * CA + 2
    offset = jnp.where(offset < 0, offset + total_rows, offset)
    offset = jnp.where(offset >= total_rows, offset - total_rows, offset)
    apart = jnp.abs(lax.broadcasted_iota(jnp.int32, (H, slots), 0) - height)
    by_height = jnp.where(apart == 0, 0.5, jnp.where(apart == 1, 0.25, 0.0))
    for i in range(ROWS):
        apart = jnp.abs(i - 1 - offset)
        by_row = jnp.where(apart == 0, 0.5, jnp.where(apart == 1, 0.25, 0.0))
        by_row = jnp.where(live, by_row, 0.0)
        weights[i * H : (i + 1) * H, :] = (by_height * by_row).astype(jnp.bfloat16)

    depth = lax.broadcasted_iota(jnp.int32, (width, 128), 0)
    lane = lax.broadcasted_iota(jnp.int32, (width, 128), 1)
    place = lane // 20
    odd = lane % 2 == 1
    mirror = jnp.where(place == 1, jnp.where(odd, width - 2, 1), jnp.where(odd, width - 1, 0))
    mirror = jnp.where(place == 2, width - 1 - mirror, mirror)
    hit = (mirror == depth) & (place < 3)
    channel = (lane % 20) // 2
    select = jnp.concatenate(
        [jnp.where(hit & (channel == c), 1.0, 0.0).astype(jnp.bfloat16) for c in range(CHANNELS)],
        axis=0,
    )

    for c in range(CHANNELS):
        loads[c].wait()
        top, rest = split(vin[c])
        high[:, c * width : (c + 1) * width] = top
        low[:, c * width : (c + 1) * width] = rest

    def dot(a, b):
        return jnp.dot(a, b, preferred_element_type=jnp.float32)

    def deposited(top, rest):
        both = dot(weights[...], jnp.concatenate([top, rest], axis=1))
        return both[:, :128] + both[:, 128:]

    strip[...] = deposited(
        dot(high[...], select).astype(jnp.bfloat16), dot(low[...], select).astype(jnp.bfloat16)
    )

    pl.semaphore_wait(
        barrier, 2 + has_outer.astype(jnp.int32) + has_inner.astype(jnp.int32)
    )
    to_outer = pltpu.make_async_remote_copy(
        src_ref=strip, dst_ref=strip_left, send_sem=band_send.at[0], recv_sem=band_recv.at[0],
        device_id={"rad": outer}, device_id_type=MESH,
    )
    to_inner = pltpu.make_async_remote_copy(
        src_ref=strip, dst_ref=strip_right, send_sem=band_send.at[1], recv_sem=band_recv.at[1],
        device_id={"rad": inner}, device_id_type=MESH,
    )

    @pl.when(has_outer)
    def _():
        to_outer.start()

    @pl.when(has_inner)
    def _():
        to_inner.start()

    sends = {}

    def send(name, source_right, target_left, source_left, target_right):
        pair = []
        for way, (source, target, device) in enumerate(
            ((source_right, target_left, right), (source_left, target_right, left))
        ):
            copy = pltpu.make_async_remote_copy(
                src_ref=source, dst_ref=target,
                send_sem=send_sem.at[way, name], recv_sem=recv_sem.at[way, name],
                device_id={"az": device}, device_id_type=MESH,
            )
            copy.start()
            pair.append(copy)
        sends[name] = pair

    def deposit_and_send(c):
        columns = slice(c * width, (c + 1) * width)
        part[c] = deposited(high[:, columns], low[:, columns])
        wide = c in WIDE
        size = SEND if wide else SEND - H
        skip = 0 if wide else H
        send(
            c,
            part.at[c, pl.ds(LINES - size, size)], from_left.at[c, pl.ds(skip, size)],
            part.at[c, pl.ds(0, size)], from_right.at[c, pl.ds(0, size)],
        )

    for c in ORDER[:FIRST]:
        deposit_and_send(c)

    @pl.when(has_inner)
    def _():
        to_outer.wait_recv()

    @pl.when(jnp.logical_not(has_inner))
    def _():
        strip_left[...] = jnp.zeros_like(strip_left)

    @pl.when(has_outer)
    def _():
        to_inner.wait_recv()

    @pl.when(jnp.logical_not(has_outer))
    def _():
        strip_right[...] = jnp.zeros_like(strip_right)

    lane = lax.broadcasted_iota(jnp.int32, (LINES, 128), 1)
    beside = jnp.where(lane % 2 == 0, strip_right[...], strip_left[...])
    edges = jnp.where(lane < 40, beside, strip[...])
    edge_out[0] = jnp.transpose(edges[LINES - SEND :])[:64]
    edge_out[1] = jnp.transpose(edges[:SEND])[:64]
    send(CHANNELS, edge_out.at[0], edge_left, edge_out.at[1], edge_right)

    for c in ORDER[FIRST:]:
        deposit_and_send(c)

    def arrived(name):
        for copy in sends[name]:
            copy.wait_recv()

    arrived(CHANNELS)
    nothing = jnp.zeros((64, 128), jnp.float32)
    edges = jnp.concatenate(
        [
            edges[2 * H : 6 * H] + jnp.transpose(jnp.concatenate([edge_left[...], nothing], axis=0)),
            edges[6 * H : 8 * H],
            edges[8 * H : 12 * H] + jnp.transpose(jnp.concatenate([edge_right[...], nothing], axis=0)),
        ],
        axis=0,
    )
    lines = (CA + 2) * H
    lane = lax.broadcasted_iota(jnp.int32, (1, 128), 1)
    inside = jnp.where(lane % 2 == 0, has_outer.astype(jnp.float32), has_inner.astype(jnp.float32))
    edge_smoothed = 0.5 * edges + 0.25 * (pltpu.roll(edges, 108, 1) + pltpu.roll(edges, 88, 1))
    edge_smoothed = edge_smoothed * inside
    edge_combined = edge_smoothed[H : H + CA * H]
    density = 1.0 / (edge_combined + density_base)
    for c in (1, 2, 3):
        own = (lane == 2 * c) | (lane == 2 * c + 1)
        edge_combined = edge_combined * jnp.where(own, pltpu.roll(density, 2 * c, 1), 1.0)

    def beside_in_band(value, edge, c):
        edge = pltpu.roll(edge, 127 - 2 * c, 1)
        return (
            jnp.where(lane == 0, edge, pltpu.roll(value, 1, 1)),
            jnp.where(lane == 127, edge, pltpu.roll(value, 127, 1)),
        )

    radius = (width * n_rad + band * width + lane).astype(jnp.float32) + 0.5
    scale_az = 0.5 / (radius * (2.0 * math.pi / total_rows))
    recip = 1.0 / radius
    cell = lax.broadcasted_iota(jnp.int32, (CA * H, 1), 0) & (H - 1)

    def smooth(c):
        arrived(c)
        if c in WIDE:
            total = jnp.concatenate(
                [
                    part[c, 2 * H : 6 * H] + from_left[c],
                    part[c, 6 * H : 8 * H],
                    part[c, 8 * H : 12 * H] + from_right[c],
                ],
                axis=0,
            )
            edge = edges
        else:
            total = jnp.concatenate(
                [
                    part[c, 3 * H : 6 * H] + from_left[c, H:],
                    part[c, 6 * H : 8 * H],
                    part[c, 8 * H : 11 * H] + from_right[c, : 3 * H],
                ],
                axis=0,
            )
            edge = edges[H : H + CA * H]
        before, after = beside_in_band(total, edge, c)
        result = 0.5 * total + 0.25 * (before + after)
        smoothed_ref[c] = result[H : H + CA * H] if c in WIDE else result
        return result

    def grad_az(value):
        return (value[2 * H :] - value[: CA * H]) * scale_az

    def center(value):
        return value[H : H + CA * H]

    def grad_rad(value, c):
        before, after = beside_in_band(value, edge_combined, c)
        return (after - before) * 0.5

    def grad_height(value):
        below = jnp.where(cell == 0, 0.0, pltpu.roll(value, 1, 0))
        above = jnp.where(cell == H - 1, 0.0, pltpu.roll(value, CA * H - 1, 0))
        return (above - below) * 0.5

    density = 1.0 / (smooth(0) + density_base)
    value = smooth(1) * density
    middle = center(value)
    strain_ref[0] = grad_az(value)
    strain_ref[3] = grad_height(middle)
    strain_ref[4] = grad_rad(middle, 1) - middle * recip
    value = smooth(2) * density
    middle = center(value)
    strain_ref[1] = grad_height(middle)
    strain_ref[3] = 0.5 * (strain_ref[3] + grad_az(value))
    strain_ref[5] = grad_rad(middle, 2)
    value = smooth(3) * density
    middle = center(value)
    strain_ref[0] += middle * recip
    strain_ref[2] = grad_rad(middle, 3)
    strain_ref[4] = 0.5 * (strain_ref[4] + grad_az(value))
    strain_ref[5] = 0.5 * (strain_ref[5] + grad_height(middle))
    value = smooth(4)
    force_ref[0] = grad_az(value)
    force_ref[2] = -center(value) * recip
    value = smooth(7)
    force_ref[0] += grad_height(center(value))
    force_ref[1] = grad_az(value)
    value = smooth(8)
    middle = center(value)
    force_ref[0] += grad_rad(middle, 8) + 2.0 * middle * recip
    force_ref[2] += grad_az(value)
    force_ref[1] += grad_height(smooth(5))
    middle = smooth(6)
    force_ref[2] += grad_rad(middle, 6) + middle * recip
    middle = smooth(9)
    force_ref[1] += grad_rad(middle, 9)
    force_ref[2] += grad_height(middle)

    for pair in sends.values():
        for copy in pair:
            copy.wait_send()

    @pl.when(has_outer)
    def _():
        to_outer.wait_send()

    @pl.when(has_inner)
    def _():
        to_inner.wait_send()


def local(block_mass, block_flux, block_dest, block_count):
    n_az = lax.axis_size("az")
    n_rad = lax.axis_size("rad")
    slots, width = block_mass.shape[2:]
    cells = CA * H
    f32 = jnp.float32
    outs = pl.pallas_call(
        functools.partial(kernel, n_az, n_rad),
        out_shape=[jax.ShapeDtypeStruct((k, cells, width), f32) for k in (CHANNELS, 3, 6)],
        in_specs=[
            pl.BlockSpec(memory_space=pltpu.SMEM),
            pl.BlockSpec(memory_space=pltpu.VMEM),
            pl.BlockSpec(memory_space=pl.ANY),
            pl.BlockSpec(memory_space=pl.ANY),
        ],
        out_specs=[pl.BlockSpec(memory_space=pltpu.VMEM)] * 3,
        scratch_shapes=[
            pltpu.VMEM((CHANNELS, slots, width), f32),
            pltpu.VMEM((slots, CHANNELS * width), jnp.bfloat16),
            pltpu.VMEM((slots, CHANNELS * width), jnp.bfloat16),
            pltpu.VMEM((LINES, slots), jnp.bfloat16),
            pltpu.VMEM((CHANNELS, LINES, width), f32),
            pltpu.VMEM((CHANNELS, SEND, width), f32),
            pltpu.VMEM((CHANNELS, SEND, width), f32),
            pltpu.VMEM((LINES, 128), f32),
            pltpu.VMEM((LINES, 128), f32),
            pltpu.VMEM((LINES, 128), f32),
            pltpu.VMEM((2, 64, SEND), f32),
            pltpu.VMEM((64, SEND), f32),
            pltpu.VMEM((64, SEND), f32),
            pltpu.SemaphoreType.DMA((CHANNELS,)),
            pltpu.SemaphoreType.DMA((2, CHANNELS + 1)),
            pltpu.SemaphoreType.DMA((2, CHANNELS + 1)),
            pltpu.SemaphoreType.DMA((2,)),
            pltpu.SemaphoreType.DMA((2,)),
        ],
        compiler_params=pltpu.CompilerParams(
            collective_id=0, has_side_effects=True, vmem_limit_bytes=40 * 1024 * 1024
        ),
    )(
        block_count,
        block_dest.reshape(1, slots),
        block_mass.reshape(slots, width),
        jnp.transpose(block_flux.reshape(slots, 9, width), (1, 0, 2)),
    )
    return tuple(out.reshape(out.shape[0], CA, H, width) for out in outs)


def solution(mesh):
    return jax.shard_map(
        local,
        mesh=mesh,
        in_specs=(
            P("az", "rad", None, None),
            P("az", "rad", None, None, None),
            P("az", "rad", None),
            P("az", "rad"),
        ),
        out_specs=(
            P(None, "az", None, "rad"),
            P(None, "az", None, "rad"),
            P(None, "az", None, "rad"),
        ),
        check_vma=False,
    )
```

time: 77 us -> 28.2 us (0.37)
  the two profiles are of different devices: /device:TPU:0 before, /device:TPU:1 now
where the time goes in v1:
time: 28.2 us; the launch traced here: 28 us
  Pallas kernels  20.7 us (73%)
  local copies, waits for them, and re-layouts  5.97 us (21%)
  between operations  1.3 us (5%)
    pallas_call x1, Pallas kernels, local(): pl.pallas_call(functools.partial(kernel, n_az, n_rad), out_shape=[jax.Sha...  20.7 us
    unnamed x9, local copies, waits for them, and re-layouts  5.97 us

profile of v1, /device:TPU:1, one launch (start us, length us, event | category | flops | bytes accessed | tf_op | source)
XLA Modules:
  0.0 28.0 jit_solution(14041434601268410628)
XLA Ops:
  1.3 0.0 copy-start
  1.3 1.7 %copy-done = f32[1,1,512,9,128]{4,2,3,1,0:T(8,128)S(1)} copy-done((f32[1,1,512,9,128]{4,2,3,1,0:T(8,128)S(1)}, f32[1,1,512,9,128]{4,2,3,1,0:T(8,128)}, u32[]{:S(2)}) %copy-start) | copy-done | bytes 2359320
  2.9 0.0 copy-start.1
  2.9 0.9 %copy-done.1 = f32[1,1,512,128]{3,2,1,0:T(8,128)S(1)} copy-done((f32[1,1,512,128]{3,2,1,0:T(8,128)S(1)}, f32[1,1,512,128]{3,2,1,0:T(8,128)}, u32[]{:S(2)}) %copy-start.1) | copy-done | bytes 262168
  3.9 0.0 copy-start.2
  3.9 0.7 %copy-done.2 = s32[1,1,512]{2,1,0:T(1,128)S(1)} copy-done((s32[1,1,512]{2,1,0:T(1,128)S(1)}, s32[1,1,512]{2,1,0:T(1,128)}, u32[]{:S(2)}) %copy-start.2) | copy-done | bytes 2072
  4.6 20.7 %shard_map.67 = (f32[10,256,128]{2,1,0:T(8,128)S(1)}, f32[3,256,128]{2,1,0:T(8,128)S(1)}, f32[6,256,128]{2,1,0:T(8,128)S(1)}) custom-call(s32[1,1]{1,0:T(1,128)S(6)} %copy.10.count_ref, s32[1,512]{1,0:T(1,128)S(1)} %bitcast.13, f32[512,128]{1,0:T(8,128)S(1)} %bitcast.12, f32[9,512,128]{2,1,0:T(8,128)S(1)} %bitcast.8), custom_call_target="tpu_custom_call" | custom-call | tf_op jit(solution)/shard_map/pallas_call | solution.py:321
  25.3 1.1 %copy.11 = f32[10,8,32,128]{3,2,1,0:T(8,128)} copy(f32[10,8,32,128]{3,2,1,0:T(8,128)S(1)} %bitcast.9) | data formatting | bytes 2621440
  26.4 0.7 %copy.12 = f32[3,8,32,128]{3,2,1,0:T(8,128)} copy(f32[3,8,32,128]{3,2,1,0:T(8,128)S(1)} %bitcast.11) | data formatting | bytes 786432
  27.1 0.9 %copy.13 = f32[6,8,32,128]{3,2,1,0:T(8,128)} copy(f32[6,8,32,128]{3,2,1,0:T(8,128)S(1)} %bitcast.10) | data formatting | bytes 1572864
Async XLA Ops:
  1.3 1.7 %copy-start = (f32[1,1,512,9,128]{4,2,3,1,0:T(8,128)S(1)}, f32[1,1,512,9,128]{4,2,3,1,0:T(8,128)}, u32[]{:S(2)}) copy-start(f32[1,1,512,9,128]{4,2,3,1,0:T(8,128)} %param.5) | copy-start | bytes 7077892
  2.9 0.9 %copy-start.1 = (f32[1,1,512,128]{3,2,1,0:T(8,128)S(1)}, f32[1,1,512,128]{3,2,1,0:T(8,128)}, u32[]{:S(2)}) copy-start(f32[1,1,512,128]{3,2,1,0:T(8,128)} %param.4) | copy-start | bytes 786436
  3.9 0.7 %copy-start.2 = (s32[1,1,512]{2,1,0:T(1,128)S(1)}, s32[1,1,512]{2,1,0:T(1,128)}, u32[]{:S(2)}) copy-start(s32[1,1,512]{2,1,0:T(1,128)} %param.6) | copy-start | bytes 6148

commit v2 on v1

--- a/solution.py
+++ b/solution.py
@@ -19,7 +19,7 @@
 
 WIDE = (0, 1, 2, 3, 4, 7, 8)
 ORDER = (0, 1, 2, 3, 4, 7, 8, 5, 6, 9)
-FIRST = 4
+EARLY, FIRST = 2, 5
 
 MESH = pl.DeviceIdType.MESH
 
@@ -31,9 +31,9 @@
 
 
 def kernel(
-    n_az, n_rad, count_ref, dest_ref, mass_ref, flux_ref,
+    n_az, n_rad, count_ref, dest_in, mass_ref, flux_ref,
     smoothed_ref, force_ref, strain_ref,
-    vin, high, low, weights, part, from_left, from_right,
+    dest_ref, vin, high, low, weights, part, from_left, from_right,
     strip, strip_left, strip_right, edge_out, edge_left, edge_right,
     load_sem, send_sem, recv_sem, band_send, band_recv,
 ):
@@ -46,12 +46,13 @@
     outer, inner = band + 1, band - 1
     has_outer, has_inner = band < n_rad - 1, band > 0
 
-    loads = []
-    for c in range(CHANNELS):
+    load_dest = pltpu.make_async_copy(dest_in, dest_ref, load_sem.at[CHANNELS])
+    load_dest.start()
+    loads = {}
+    for c in ORDER:
         source = mass_ref if c == 0 else flux_ref.at[c - 1]
-        copy = pltpu.make_async_copy(source, vin.at[c], load_sem.at[c])
-        copy.start()
-        loads.append(copy)
+        loads[c] = pltpu.make_async_copy(source, vin.at[c], load_sem.at[c])
+        loads[c].start()
 
     barrier = pltpu.get_barrier_semaphore()
     for neighbour in (left, right):
@@ -65,6 +66,7 @@
     def _():
         pl.semaphore_signal(barrier, inc=1, device_id={"rad": inner}, device_id_type=MESH)
 
+    load_dest.wait()
     dest = dest_ref[...]
     live = lax.broadcasted_iota(jnp.int32, (1, slots), 1) < count_ref[0, 0]
     height = dest & (H - 1)
@@ -79,20 +81,7 @@
         by_row = jnp.where(live, by_row, 0.0)
         weights[i * H : (i + 1) * H, :] = (by_height * by_row).astype(jnp.bfloat16)
 
-    depth = lax.broadcasted_iota(jnp.int32, (width, 128), 0)
-    lane = lax.broadcasted_iota(jnp.int32, (width, 128), 1)
-    place = lane // 20
-    odd = lane % 2 == 1
-    mirror = jnp.where(place == 1, jnp.where(odd, width - 2, 1), jnp.where(odd, width - 1, 0))
-    mirror = jnp.where(place == 2, width - 1 - mirror, mirror)
-    hit = (mirror == depth) & (place < 3)
-    channel = (lane % 20) // 2
-    select = jnp.concatenate(
-        [jnp.where(hit & (channel == c), 1.0, 0.0).astype(jnp.bfloat16) for c in range(CHANNELS)],
-        axis=0,
-    )
-
-    for c in range(CHANNELS):
+    def unpack(c):
         loads[c].wait()
         top, rest = split(vin[c])
         high[:, c * width : (c + 1) * width] = top
@@ -104,30 +93,6 @@
     def deposited(top, rest):
         both = dot(weights[...], jnp.concatenate([top, rest], axis=1))
         return both[:, :128] + both[:, 128:]
-
-    strip[...] = deposited(
-        dot(high[...], select).astype(jnp.bfloat16), dot(low[...], select).astype(jnp.bfloat16)
-    )
-
-    pl.semaphore_wait(
-        barrier, 2 + has_outer.astype(jnp.int32) + has_inner.astype(jnp.int32)
-    )
-    to_outer = pltpu.make_async_remote_copy(
-        src_ref=strip, dst_ref=strip_left, send_sem=band_send.at[0], recv_sem=band_recv.at[0],
-        device_id={"rad": outer}, device_id_type=MESH,
-    )
-    to_inner = pltpu.make_async_remote_copy(
-        src_ref=strip, dst_ref=strip_right, send_sem=band_send.at[1], recv_sem=band_recv.at[1],
-        device_id={"rad": inner}, device_id_type=MESH,
-    )
-
-    @pl.when(has_outer)
-    def _():
-        to_outer.start()
-
-    @pl.when(has_inner)
-    def _():
-        to_inner.start()
 
     sends = {}
 
@@ -145,9 +110,11 @@
             pair.append(copy)
         sends[name] = pair
 
-    def deposit_and_send(c):
+    def deposit(c):
         columns = slice(c * width, (c + 1) * width)
         part[c] = deposited(high[:, columns], low[:, columns])
+
+    def send_channel(c):
         wide = c in WIDE
         size = SEND if wide else SEND - H
         skip = 0 if wide else H
@@ -157,8 +124,55 @@
             part.at[c, pl.ds(0, size)], from_right.at[c, pl.ds(0, size)],
         )
 
-    for c in ORDER[:FIRST]:
-        deposit_and_send(c)
+    for c in ORDER[:EARLY]:
+        unpack(c)
+        deposit(c)
+        if c == ORDER[0]:
+            pl.semaphore_wait(
+                barrier, 2 + has_outer.astype(jnp.int32) + has_inner.astype(jnp.int32)
+            )
+        send_channel(c)
+    for c in ORDER[EARLY:]:
+        unpack(c)
+
+    depth = lax.broadcasted_iota(jnp.int32, (width, 128), 0)
+    lane = lax.broadcasted_iota(jnp.int32, (width, 128), 1)
+    place = lane // 20
+    odd = lane % 2 == 1
+    mirror = jnp.where(place == 1, jnp.where(odd, width - 2, 1), jnp.where(odd, width - 1, 0))
+    mirror = jnp.where(place == 2, width - 1 - mirror, mirror)
+    hit = (mirror == depth) & (place < 3)
+    channel = (lane % 20) // 2
+    select = jnp.concatenate(
+        [jnp.where(hit & (channel == c), 1.0, 0.0).astype(jnp.bfloat16) for c in range(CHANNELS)],
+        axis=0,
+    )
+
+    strip[...] = deposited(
+        dot(high[...], select).astype(jnp.bfloat16), dot(low[...], select).astype(jnp.bfloat16)
+    )
+    to_outer = pltpu.make_async_remote_copy(
+        src_ref=strip, dst_ref=strip_left, send_sem=band_send.at[0], recv_sem=band_recv.at[0],
+        device_id={"rad": outer}, device_id_type=MESH,
+    )
+    to_inner = pltpu.make_async_remote_copy(
+        src_ref=strip, dst_ref=strip_right, send_sem=band_send.at[1], recv_sem=band_recv.at[1],
+        device_id={"rad": inner}, device_id_type=MESH,
+    )
+
+    @pl.when(has_outer)
+    def _():
+        to_outer.start()
+
+    @pl.when(has_inner)
+    def _():
+        to_inner.start()
+
+    for c in ORDER[EARLY:FIRST]:
+        deposit(c)
+        send_channel(c)
+    for c in ORDER[FIRST:]:
+        deposit(c)
 
     @pl.when(has_inner)
     def _():
@@ -184,7 +198,7 @@
     send(CHANNELS, edge_out.at[0], edge_left, edge_out.at[1], edge_right)
 
     for c in ORDER[FIRST:]:
-        deposit_and_send(c)
+        send_channel(c)
 
     def arrived(name):
         for copy in sends[name]:
@@ -312,6 +326,25 @@
         to_inner.wait_send()
 
 
+def store(smoothed, force, strain, smoothed_out, force_out, strain_out, sem):
+    half = CHANNELS // 2
+    copies = [
+        pltpu.make_async_copy(source, target, sem.at[i])
+        for i, (source, target) in enumerate(
+            (
+                (smoothed.at[pl.ds(0, half)], smoothed_out.at[pl.ds(0, half)]),
+                (smoothed.at[pl.ds(half, half)], smoothed_out.at[pl.ds(half, half)]),
+                (strain, strain_out),
+                (force, force_out),
+            )
+        )
+    ]
+    for copy in copies:
+        copy.start()
+    for copy in copies:
+        copy.wait()
+
+
 def local(block_mass, block_flux, block_dest, block_count):
     n_az = lax.axis_size("az")
     n_rad = lax.axis_size("rad")
@@ -320,15 +353,16 @@
     f32 = jnp.float32
     outs = pl.pallas_call(
         functools.partial(kernel, n_az, n_rad),
-        out_shape=[jax.ShapeDtypeStruct((k, cells, width), f32) for k in (CHANNELS, 3, 6)],
+        out_shape=[pltpu.VMEM((k, cells, width), f32) for k in (CHANNELS, 3, 6)],
         in_specs=[
             pl.BlockSpec(memory_space=pltpu.SMEM),
-            pl.BlockSpec(memory_space=pltpu.VMEM),
+            pl.BlockSpec(memory_space=pl.ANY),
             pl.BlockSpec(memory_space=pl.ANY),
             pl.BlockSpec(memory_space=pl.ANY),
         ],
         out_specs=[pl.BlockSpec(memory_space=pltpu.VMEM)] * 3,
         scratch_shapes=[
+            pltpu.VMEM((1, slots), jnp.int32),
             pltpu.VMEM((CHANNELS, slots, width), f32),
             pltpu.VMEM((slots, CHANNELS * width), jnp.bfloat16),
             pltpu.VMEM((slots, CHANNELS * width), jnp.bfloat16),
@@ -342,14 +376,14 @@
             pltpu.VMEM((2, 64, SEND), f32),
             pltpu.VMEM((64, SEND), f32),
             pltpu.VMEM((64, SEND), f32),
-            pltpu.SemaphoreType.DMA((CHANNELS,)),
+            pltpu.SemaphoreType.DMA((CHANNELS + 1,)),
             pltpu.SemaphoreType.DMA((2, CHANNELS + 1)),
             pltpu.SemaphoreType.DMA((2, CHANNELS + 1)),
             pltpu.SemaphoreType.DMA((2,)),
             pltpu.SemaphoreType.DMA((2,)),
         ],
         compiler_params=pltpu.CompilerParams(
-            collective_id=0, has_side_effects=True, vmem_limit_bytes=40 * 1024 * 1024
+            collective_id=0, has_side_effects=True, vmem_limit_bytes=56 * 1024 * 1024
         ),
     )(
         block_count,
@@ -357,6 +391,14 @@
         block_mass.reshape(slots, width),
         jnp.transpose(block_flux.reshape(slots, 9, width), (1, 0, 2)),
     )
+    outs = pl.pallas_call(
+        store,
+        out_shape=[jax.ShapeDtypeStruct((k, cells, width), f32) for k in (CHANNELS, 3, 6)],
+        in_specs=[pl.BlockSpec(memory_space=pltpu.VMEM)] * 3,
+        out_specs=[pl.BlockSpec(memory_space=pltpu.HBM)] * 3,
+        scratch_shapes=[pltpu.SemaphoreType.DMA((4,))],
+        compiler_params=pltpu.CompilerParams(vmem_limit_bytes=8 * 1024 * 1024),
+    )(*outs)
     return tuple(out.reshape(out.shape[0], CA, H, width) for out in outs)
 
 

time: 28.2 us -> 24.1 us (0.85)
  local copies, waits for them, and re-layouts: 5.97 us -> 0 us
  Pallas kernels: 20.7 us -> 22.6 us
    unnamed x9 -> x0, local copies, waits for them, and re-layouts: 5.97 us -> none
    pallas_call x1 -> x2, Pallas kernels: 20.7 us -> 22.6 us  [the longest x1 21.1 us: local(): pl.pallas_call(functools.partial(kernel, n_az, n_rad), out_shape=[pltpu.V...]
where the time goes in v2:
time: 24.1 us; the launch traced here: 23.9 us
  Pallas kernels  22.6 us (94%)
  between operations  1.29 us (5%)
    pallas_call x1, Pallas kernels, local(): pl.pallas_call(functools.partial(kernel, n_az, n_rad), out_shape=[pltpu.V...  21.1 us
    pallas_call x1, Pallas kernels, local(): pl.pallas_call(store, out_shape=[jax.ShapeDtypeStruct((k, cells, width),...  1.47 us

profile of v2, /device:TPU:1, one launch (start us, length us, event | category | flops | bytes accessed | tf_op | source)
XLA Modules:
  0.0 23.9 jit_solution(14767871045457266772)
XLA Ops:
  1.3 21.1 %shard_map.67 = (f32[10,256,128]{2,1,0:T(8,128)S(1)}, f32[3,256,128]{2,1,0:T(8,128)S(1)}, f32[6,256,128]{2,1,0:T(8,128)S(1)}) custom-call(s32[1,1]{1,0:T(1,128)S(6)} %copy.7.count_ref, s32[1,512]{1,0:T(1,128)} %bitcast.10, f32[512,128]{1,0:T(8,128)} %bitcast.9, f32[9,512,128]{2,1,0:T(8,128)} %bitcast.8), custom_call_target="tpu_custom_call" | custom-call | tf_op jit(solution)/shard_map/pallas_call | solution.py:354
  22.4 1.5 %shard_map.68 = (f32[10,256,128]{2,1,0:T(8,128)}, f32[3,256,128]{2,1,0:T(8,128)}, f32[6,256,128]{2,1,0:T(8,128)}) custom-call(f32[10,256,128]{2,1,0:T(8,128)S(1)} %get-tuple-element.9.smoothed, f32[3,256,128]{2,1,0:T(8,128)S(1)} %get-tuple-element.10.force, f32[6,256,128]{2,1,0:T(8,128)S(1)} %get-tuple-element.11.strain), custom_call_target="tpu_custom_call" | custom-call | tf_op jit(solution)/shard_map/pallas_call | solution.py:394

commit v3 on v2

--- a/solution.py
+++ b/solution.py
@@ -14,10 +14,12 @@
 ROWS = CA + 6
 LINES = ROWS * H
 SEND = 4 * H
+EDGES = 4 * CHANNELS
 
 density_base = 0.5
 
 WIDE = (0, 1, 2, 3, 4, 7, 8)
+RADIAL = (0, 1, 2, 3, 6, 8, 9)
 ORDER = (0, 1, 2, 3, 4, 7, 8, 5, 6, 9)
 EARLY, FIRST = 2, 5
 
@@ -140,8 +142,7 @@
     place = lane // 20
     odd = lane % 2 == 1
     mirror = jnp.where(place == 1, jnp.where(odd, width - 2, 1), jnp.where(odd, width - 1, 0))
-    mirror = jnp.where(place == 2, width - 1 - mirror, mirror)
-    hit = (mirror == depth) & (place < 3)
+    hit = (mirror == depth) & (place < 2)
     channel = (lane % 20) // 2
     select = jnp.concatenate(
         [jnp.where(hit & (channel == c), 1.0, 0.0).astype(jnp.bfloat16) for c in range(CHANNELS)],
@@ -191,10 +192,9 @@
         strip_right[...] = jnp.zeros_like(strip_right)
 
     lane = lax.broadcasted_iota(jnp.int32, (LINES, 128), 1)
-    beside = jnp.where(lane % 2 == 0, strip_right[...], strip_left[...])
-    edges = jnp.where(lane < 40, beside, strip[...])
-    edge_out[0] = jnp.transpose(edges[LINES - SEND :])[:64]
-    edge_out[1] = jnp.transpose(edges[:SEND])[:64]
+    edges = jnp.where(lane % 2 == 0, strip_right[...], strip_left[...])
+    edge_out[0] = jnp.transpose(edges[LINES - SEND :])[:EDGES]
+    edge_out[1] = jnp.transpose(edges[:SEND])[:EDGES]
     send(CHANNELS, edge_out.at[0], edge_left, edge_out.at[1], edge_right)
 
     for c in ORDER[FIRST:]:
@@ -205,7 +205,7 @@
             copy.wait_recv()
 
     arrived(CHANNELS)
-    nothing = jnp.zeros((64, 128), jnp.float32)
+    nothing = jnp.zeros((128 - EDGES, 128), jnp.float32)
     edges = jnp.concatenate(
         [
             edges[2 * H : 6 * H] + jnp.transpose(jnp.concatenate([edge_left[...], nothing], axis=0)),
@@ -214,19 +214,10 @@
         ],
         axis=0,
     )
-    lines = (CA + 2) * H
     lane = lax.broadcasted_iota(jnp.int32, (1, 128), 1)
-    inside = jnp.where(lane % 2 == 0, has_outer.astype(jnp.float32), has_inner.astype(jnp.float32))
-    edge_smoothed = 0.5 * edges + 0.25 * (pltpu.roll(edges, 108, 1) + pltpu.roll(edges, 88, 1))
-    edge_smoothed = edge_smoothed * inside
-    edge_combined = edge_smoothed[H : H + CA * H]
-    density = 1.0 / (edge_combined + density_base)
-    for c in (1, 2, 3):
-        own = (lane == 2 * c) | (lane == 2 * c + 1)
-        edge_combined = edge_combined * jnp.where(own, pltpu.roll(density, 2 * c, 1), 1.0)
-
-    def beside_in_band(value, edge, c):
-        edge = pltpu.roll(edge, 127 - 2 * c, 1)
+    inside = jnp.where(lane == 0, has_inner.astype(jnp.float32), has_outer.astype(jnp.float32))
+
+    def beside_in_band(value, edge):
         return (
             jnp.where(lane == 0, edge, pltpu.roll(value, 1, 1)),
             jnp.where(lane == 127, edge, pltpu.roll(value, 127, 1)),
@@ -259,10 +250,16 @@
                 axis=0,
             )
             edge = edges[H : H + CA * H]
-        before, after = beside_in_band(total, edge, c)
+        near = pltpu.roll(edge, 127 - 2 * c, 1)
+        before, after = beside_in_band(total, near)
         result = 0.5 * total + 0.25 * (before + after)
-        smoothed_ref[c] = result[H : H + CA * H] if c in WIDE else result
-        return result
+        smoothed_ref[c] = center(result) if c in WIDE else result
+        if c not in RADIAL:
+            return result
+        if c in WIDE:
+            edge, near, total = center(edge), center(near), center(total)
+        far = pltpu.roll(edge, 107 - 2 * c, 1)
+        return result, (0.5 * near + 0.25 * (far + total)) * inside
 
     def grad_az(value):
         return (value[2 * H :] - value[: CA * H]) * scale_az
@@ -270,8 +267,8 @@
     def center(value):
         return value[H : H + CA * H]
 
-    def grad_rad(value, c):
-        before, after = beside_in_band(value, edge_combined, c)
+    def grad_rad(value, edge):
+        before, after = beside_in_band(value, edge)
         return (after - before) * 0.5
 
     def grad_height(value):
@@ -279,21 +276,25 @@
         above = jnp.where(cell == H - 1, 0.0, pltpu.roll(value, CA * H - 1, 0))
         return (above - below) * 0.5
 
-    density = 1.0 / (smooth(0) + density_base)
-    value = smooth(1) * density
+    value, edge = smooth(0)
+    density, edge_density = 1.0 / (value + density_base), 1.0 / (edge + density_base)
+    value, edge = smooth(1)
+    value, edge = value * density, edge * edge_density
     middle = center(value)
     strain_ref[0] = grad_az(value)
     strain_ref[3] = grad_height(middle)
-    strain_ref[4] = grad_rad(middle, 1) - middle * recip
-    value = smooth(2) * density
+    strain_ref[4] = grad_rad(middle, edge) - middle * recip
+    value, edge = smooth(2)
+    value, edge = value * density, edge * edge_density
     middle = center(value)
     strain_ref[1] = grad_height(middle)
     strain_ref[3] = 0.5 * (strain_ref[3] + grad_az(value))
-    strain_ref[5] = grad_rad(middle, 2)
-    value = smooth(3) * density
+    strain_ref[5] = grad_rad(middle, edge)
+    value, edge = smooth(3)
+    value, edge = value * density, edge * edge_density
     middle = center(value)
     strain_ref[0] += middle * recip
-    strain_ref[2] = grad_rad(middle, 3)
+    strain_ref[2] = grad_rad(middle, edge)
     strain_ref[4] = 0.5 * (strain_ref[4] + grad_az(value))
     strain_ref[5] = 0.5 * (strain_ref[5] + grad_height(middle))
     value = smooth(4)
@@ -302,15 +303,15 @@
     value = smooth(7)
     force_ref[0] += grad_height(center(value))
     force_ref[1] = grad_az(value)
-    value = smooth(8)
+    value, edge = smooth(8)
     middle = center(value)
-    force_ref[0] += grad_rad(middle, 8) + 2.0 * middle * recip
+    force_ref[0] += grad_rad(middle, edge) + 2.0 * middle * recip
     force_ref[2] += grad_az(value)
     force_ref[1] += grad_height(smooth(5))
-    middle = smooth(6)
-    force_ref[2] += grad_rad(middle, 6) + middle * recip
-    middle = smooth(9)
-    force_ref[1] += grad_rad(middle, 9)
+    middle, edge = smooth(6)
+    force_ref[2] += grad_rad(middle, edge) + middle * recip
+    middle, edge = smooth(9)
+    force_ref[1] += grad_rad(middle, edge)
     force_ref[2] += grad_height(middle)
 
     for pair in sends.values():
@@ -327,20 +328,12 @@
 
 
 def store(smoothed, force, strain, smoothed_out, force_out, strain_out, sem):
-    half = CHANNELS // 2
-    copies = [
-        pltpu.make_async_copy(source, target, sem.at[i])
-        for i, (source, target) in enumerate(
-            (
-                (smoothed.at[pl.ds(0, half)], smoothed_out.at[pl.ds(0, half)]),
-                (smoothed.at[pl.ds(half, half)], smoothed_out.at[pl.ds(half, half)]),
-                (strain, strain_out),
-                (force, force_out),
-            )
-        )
-    ]
-    for copy in copies:
-        copy.start()
+    copies = []
+    for source, target in ((smoothed, smoothed_out), (strain, strain_out), (force, force_out)):
+        for k in range(source.shape[0]):
+            copy = pltpu.make_async_copy(source.at[k], target.at[k], sem.at[len(copies)])
+            copy.start()
+            copies.append(copy)
     for copy in copies:
         copy.wait()
 
@@ -373,9 +366,9 @@
             pltpu.VMEM((LINES, 128), f32),
             pltpu.VMEM((LINES, 128), f32),
             pltpu.VMEM((LINES, 128), f32),
-            pltpu.VMEM((2, 64, SEND), f32),
-            pltpu.VMEM((64, SEND), f32),
-            pltpu.VMEM((64, SEND), f32),
+            pltpu.VMEM((2, EDGES, SEND), f32),
+            pltpu.VMEM((EDGES, SEND), f32),
+            pltpu.VMEM((EDGES, SEND), f32),
             pltpu.SemaphoreType.DMA((CHANNELS + 1,)),
             pltpu.SemaphoreType.DMA((2, CHANNELS + 1)),
             pltpu.SemaphoreType.DMA((2, CHANNELS + 1)),
@@ -396,7 +389,7 @@
         out_shape=[jax.ShapeDtypeStruct((k, cells, width), f32) for k in (CHANNELS, 3, 6)],
         in_specs=[pl.BlockSpec(memory_space=pltpu.VMEM)] * 3,
         out_specs=[pl.BlockSpec(memory_space=pltpu.HBM)] * 3,
-        scratch_shapes=[pltpu.SemaphoreType.DMA((4,))],
+        scratch_shapes=[pltpu.SemaphoreType.DMA((CHANNELS + 9,))],
         compiler_params=pltpu.CompilerParams(vmem_limit_bytes=8 * 1024 * 1024),
     )(*outs)
     return tuple(out.reshape(out.shape[0], CA, H, width) for out in outs)

time: 24.1 us -> 23.9 us (level)
    pallas_call x1, Pallas kernels: 21.1 us -> 20.9 us  [local(): pl.pallas_call(functools.partial(kernel, n_az, n_rad), out_shape=[pltpu.V...]
where the time goes in v3:
time: 23.9 us; the launch traced here: 23.8 us
  Pallas kernels  22.5 us (94%)
  between operations  1.29 us (5%)
    pallas_call x1, Pallas kernels, local(): pl.pallas_call(functools.partial(kernel, n_az, n_rad), out_shape=[pltpu.V...  20.9 us
    pallas_call x1, Pallas kernels, local(): pl.pallas_call(store, out_shape=[jax.ShapeDtypeStruct((k, cells, width),...  1.6 us

profile of v3, /device:TPU:1, one launch (start us, length us, event | category | flops | bytes accessed | tf_op | source)
XLA Modules:
  0.0 23.8 jit_solution(4918442603000762474)
XLA Ops:
  1.3 20.9 %shard_map.67 = (f32[10,256,128]{2,1,0:T(8,128)S(1)}, f32[3,256,128]{2,1,0:T(8,128)S(1)}, f32[6,256,128]{2,1,0:T(8,128)S(1)}) custom-call(s32[1,1]{1,0:T(1,128)S(6)} %copy.7.count_ref, s32[1,512]{1,0:T(1,128)} %bitcast.10, f32[512,128]{1,0:T(8,128)} %bitcast.9, f32[9,512,128]{2,1,0:T(8,128)} %bitcast.8), custom_call_target="tpu_custom_call" | custom-call | tf_op jit(solution)/shard_map/pallas_call | solution.py:347
  22.2 1.6 %shard_map.68 = (f32[10,256,128]{2,1,0:T(8,128)}, f32[3,256,128]{2,1,0:T(8,128)}, f32[6,256,128]{2,1,0:T(8,128)}) custom-call(f32[10,256,128]{2,1,0:T(8,128)S(1)} %get-tuple-element.9.smoothed, f32[3,256,128]{2,1,0:T(8,128)S(1)} %get-tuple-element.10.force, f32[6,256,128]{2,1,0:T(8,128)S(1)} %get-tuple-element.11.strain), custom_call_target="tpu_custom_call" | custom-call | tf_op jit(solution)/shard_map/pallas_call | solution.py:387

commit v4 on v3

--- a/solution.py
+++ b/solution.py
@@ -21,7 +21,7 @@
 WIDE = (0, 1, 2, 3, 4, 7, 8)
 RADIAL = (0, 1, 2, 3, 6, 8, 9)
 ORDER = (0, 1, 2, 3, 4, 7, 8, 5, 6, 9)
-EARLY, FIRST = 2, 5
+EARLY, FIRST = 2, 8
 
 MESH = pl.DeviceIdType.MESH
 
@@ -328,12 +328,20 @@
 
 
 def store(smoothed, force, strain, smoothed_out, force_out, strain_out, sem):
-    copies = []
-    for source, target in ((smoothed, smoothed_out), (strain, strain_out), (force, force_out)):
-        for k in range(source.shape[0]):
-            copy = pltpu.make_async_copy(source.at[k], target.at[k], sem.at[len(copies)])
-            copy.start()
-            copies.append(copy)
+    half = CHANNELS // 2
+    copies = [
+        pltpu.make_async_copy(source, target, sem.at[i])
+        for i, (source, target) in enumerate(
+            (
+                (smoothed.at[pl.ds(0, half)], smoothed_out.at[pl.ds(0, half)]),
+                (smoothed.at[pl.ds(half, half)], smoothed_out.at[pl.ds(half, half)]),
+                (strain, strain_out),
+                (force, force_out),
+            )
+        )
+    ]
+    for copy in copies:
+        copy.start()
     for copy in copies:
         copy.wait()
 
@@ -389,7 +397,7 @@
         out_shape=[jax.ShapeDtypeStruct((k, cells, width), f32) for k in (CHANNELS, 3, 6)],
         in_specs=[pl.BlockSpec(memory_space=pltpu.VMEM)] * 3,
         out_specs=[pl.BlockSpec(memory_space=pltpu.HBM)] * 3,
-        scratch_shapes=[pltpu.SemaphoreType.DMA((CHANNELS + 9,))],
+        scratch_shapes=[pltpu.SemaphoreType.DMA((4,))],
         compiler_params=pltpu.CompilerParams(vmem_limit_bytes=8 * 1024 * 1024),
     )(*outs)
     return tuple(out.reshape(out.shape[0], CA, H, width) for out in outs)

time: 23.9 us -> 23.3 us (0.975)
  Pallas kernels: 22.5 us -> 21.8 us
    pallas_call x1, Pallas kernels: 20.9 us -> 20.4 us  [local(): pl.pallas_call(functools.partial(kernel, n_az, n_rad), out_shape=[pltpu.V...]
where the time goes in v4:
time: 23.3 us; the launch traced here: 23.1 us
  Pallas kernels  21.8 us (94%)
  between operations  1.29 us (6%)
    pallas_call x1, Pallas kernels, local(): pl.pallas_call(functools.partial(kernel, n_az, n_rad), out_shape=[pltpu.V...  20.4 us
    pallas_call x1, Pallas kernels, local(): pl.pallas_call(store, out_shape=[jax.ShapeDtypeStruct((k, cells, width),...  1.47 us

profile of v4, /device:TPU:1, one launch (start us, length us, event | category | flops | bytes accessed | tf_op | source)
XLA Modules:
  0.0 23.1 jit_solution(16443557366800722407)
XLA Ops:
  1.3 20.4 %shard_map.67 = (f32[10,256,128]{2,1,0:T(8,128)S(1)}, f32[3,256,128]{2,1,0:T(8,128)S(1)}, f32[6,256,128]{2,1,0:T(8,128)S(1)}) custom-call(s32[1,1]{1,0:T(1,128)S(6)} %copy.7.count_ref, s32[1,512]{1,0:T(1,128)} %bitcast.10, f32[512,128]{1,0:T(8,128)} %bitcast.9, f32[9,512,128]{2,1,0:T(8,128)} %bitcast.8), custom_call_target="tpu_custom_call" | custom-call | tf_op jit(solution)/shard_map/pallas_call | solution.py:355
  21.6 1.5 %shard_map.68 = (f32[10,256,128]{2,1,0:T(8,128)}, f32[3,256,128]{2,1,0:T(8,128)}, f32[6,256,128]{2,1,0:T(8,128)}) custom-call(f32[10,256,128]{2,1,0:T(8,128)S(1)} %get-tuple-element.9.smoothed, f32[3,256,128]{2,1,0:T(8,128)S(1)} %get-tuple-element.10.force, f32[6,256,128]{2,1,0:T(8,128)S(1)} %get-tuple-element.11.strain), custom_call_target="tpu_custom_call" | custom-call | tf_op jit(solution)/shard_map/pallas_call | solution.py:395

commit v5 on v4

--- a/solution.py
+++ b/solution.py
@@ -21,7 +21,7 @@
 WIDE = (0, 1, 2, 3, 4, 7, 8)
 RADIAL = (0, 1, 2, 3, 6, 8, 9)
 ORDER = (0, 1, 2, 3, 4, 7, 8, 5, 6, 9)
-EARLY, FIRST = 2, 8
+EARLY, FIRST = 4, 8
 
 MESH = pl.DeviceIdType.MESH
 

time: 23.3 us -> 23.5 us (level)
  no operation moved by 1% of the time
where the time goes in v5:
time: 23.5 us; the launch traced here: 23.3 us
  Pallas kernels  22 us (94%)
  between operations  1.29 us (5%)
    pallas_call x1, Pallas kernels, local(): pl.pallas_call(functools.partial(kernel, n_az, n_rad), out_shape=[pltpu.V...  20.5 us
    pallas_call x1, Pallas kernels, local(): pl.pallas_call(store, out_shape=[jax.ShapeDtypeStruct((k, cells, width),...  1.47 us

profile of v5, /device:TPU:1, one launch (start us, length us, event | category | flops | bytes accessed | tf_op | source)
XLA Modules:
  0.0 23.3 jit_solution(8874372267448232487)
XLA Ops:
  1.3 20.5 %shard_map.67 = (f32[10,256,128]{2,1,0:T(8,128)S(1)}, f32[3,256,128]{2,1,0:T(8,128)S(1)}, f32[6,256,128]{2,1,0:T(8,128)S(1)}) custom-call(s32[1,1]{1,0:T(1,128)S(6)} %copy.7.count_ref, s32[1,512]{1,0:T(1,128)} %bitcast.10, f32[512,128]{1,0:T(8,128)} %bitcast.9, f32[9,512,128]{2,1,0:T(8,128)} %bitcast.8), custom_call_target="tpu_custom_call" | custom-call | tf_op jit(solution)/shard_map/pallas_call | solution.py:355
  21.8 1.5 %shard_map.68 = (f32[10,256,128]{2,1,0:T(8,128)}, f32[3,256,128]{2,1,0:T(8,128)}, f32[6,256,128]{2,1,0:T(8,128)}) custom-call(f32[10,256,128]{2,1,0:T(8,128)S(1)} %get-tuple-element.9.smoothed, f32[3,256,128]{2,1,0:T(8,128)S(1)} %get-tuple-element.10.force, f32[6,256,128]{2,1,0:T(8,128)S(1)} %get-tuple-element.11.strain), custom_call_target="tpu_custom_call" | custom-call | tf_op jit(solution)/shard_map/pallas_call | solution.py:395
